TPU v7x, 32 devices: a whole 2x2x4 slice. The times are simulated.
32 devices in a mesh: ctx: 8 (over z, y), fsdp: 4 (over x, core).
Axes of the slice: x: 2, y: 2, z: 4, core: 2. Of those that a mesh axis runs over, the one named last changes fastest.
Arguments:
- inputs: bfloat16 [16, 1024, 640], P('fsdp', 'ctx'), may hold values from -6 to 6
- cotangent: bfloat16 [16, 1024, 640], P('fsdp', 'ctx'), may hold values from -6 to 6
- lengths: int32 [16], P('fsdp'), may hold values from 256 to 1024, as said below
- query_weight: bfloat16 [640, 1024], P('fsdp'), may hold values from -0.25 to 0.25
- key_weight: bfloat16 [640, 256], P('fsdp'), may hold values from -0.25 to 0.25
- value_weight: bfloat16 [640, 256], P('fsdp'), may hold values from -0.25 to 0.25
- out_weight: bfloat16 [1024, 640], P('fsdp'), may hold values from -0.1875 to 0.1875
- gate_weight: bfloat16 [640, 2048], P('fsdp'), may hold values from -0.25 to 0.25
- up_weight: bfloat16 [640, 2048], P('fsdp'), may hold values from -0.25 to 0.25
- down_weight: bfloat16 [2048, 640], P('fsdp'), may hold values from -0.125 to 0.125
- pre_attn_gain: bfloat16 [640], P('fsdp'), may hold values from -0.5 to 0.5
- post_attn_gain: bfloat16 [640], P('fsdp'), may hold values from -0.5 to 0.5
- pre_ffw_gain: bfloat16 [640], P('fsdp'), may hold values from -0.5 to 0.5
- post_ffw_gain: bfloat16 [640], P('fsdp'), may hold values from -0.5 to 0.5
- query_gain: bfloat16 [256], P('fsdp'), may hold values from 0 to 0.796875
- key_gain: bfloat16 [256], P('fsdp'), may hold values from 0 to 0.796875
Outputs:
- outputs: bfloat16 [16, 1024, 640], P('fsdp', 'ctx')
- input_grad: bfloat16 [16, 1024, 640], P('fsdp', 'ctx')
- query_weight_grad: float32 [640, 1024], P('fsdp')
- key_weight_grad: float32 [640, 256], P('fsdp')
- value_weight_grad: float32 [640, 256], P('fsdp')
- out_weight_grad: float32 [1024, 640], P('fsdp')
- gate_weight_grad: float32 [640, 2048], P('fsdp')
- up_weight_grad: float32 [640, 2048], P('fsdp')
- down_weight_grad: float32 [2048, 640], P('fsdp')
- pre_attn_gain_grad: float32 [640], P('fsdp')
- post_attn_gain_grad: float32 [640], P('fsdp')
- pre_ffw_gain_grad: float32 [640], P('fsdp')
- post_ffw_gain_grad: float32 [640], P('fsdp')
- query_gain_grad: float32 [256], P('fsdp')
- key_gain_grad: float32 [256], P('fsdp')
Inputs may be any that keep to these rules, and one draw needn't show every extreme that they name: Sequence s has its first lengths[s] positions live; later keys are excluded from every softmax. In each aligned block of 4 sequences exactly one, drawn from the seed, has all 1024 positions live.
All inputs are finite; a program needn't handle non-finite values.
Results may differ from a plain program's by a relative error of at most 0.022.
Values may be sent and summed in bfloat16 or wider, within the bound.
A program may use at most 256 MiB of HBM per device.

v0:
```python
import math
import jax
import jax.numpy as jnp
from jax import lax
from jax.sharding import PartitionSpec as P

EPSILON = 1e-06
MASKED_SCORE = -1e30
ROPE_BASE = 1000000.0


def norm_gain(values, gain_vec):
    return (
        values
        * lax.rsqrt(jnp.mean(values * values, axis=-1, keepdims=True) + EPSILON)
        * (1.0 + gain_vec)
    )


def rotate(values, positions):
    half_dim = values.shape[-1] // 2
    inverse = ROPE_BASE ** (-(jnp.arange(half_dim).astype(jnp.float32) * 2.0) / values.shape[-1])
    angles = positions.astype(jnp.float32)[:, None] * inverse[None, :]
    cosine = jnp.cos(angles)[:, None, :]
    sine_part = jnp.sin(angles)[:, None, :]
    first_half = values[..., :half_dim]
    second_half = values[..., half_dim:]
    return jnp.concatenate(
        [
            first_half * cosine - second_half * sine_part,
            second_half * cosine + first_half * sine_part,
        ],
        axis=-1,
    )


def gelu_mix(gate_in, up_in):
    return jax.nn.gelu(gate_in, approximate=True) * up_in


def body(
    inputs,
    cotangent,
    lengths,
    query_weight,
    key_weight,
    value_weight,
    out_weight,
    gate_weight,
    up_weight,
    down_weight,
    pre_attn_gain,
    post_attn_gain,
    pre_ffw_gain,
    post_ffw_gain,
    query_gain,
    key_gain,
):
    seq_count, row_count, model_width = inputs.shape
    gathered = (
        lax.all_gather(query_weight, "fsdp", axis=0, tiled=True),
        lax.all_gather(key_weight, "fsdp", axis=0, tiled=True),
        lax.all_gather(value_weight, "fsdp", axis=0, tiled=True),
        lax.all_gather(out_weight, "fsdp", axis=0, tiled=True),
        lax.all_gather(gate_weight, "fsdp", axis=0, tiled=True),
        lax.all_gather(up_weight, "fsdp", axis=0, tiled=True),
        lax.all_gather(down_weight, "fsdp", axis=0, tiled=True),
        lax.all_gather(pre_attn_gain, "fsdp", axis=0, tiled=True),
        lax.all_gather(post_attn_gain, "fsdp", axis=0, tiled=True),
        lax.all_gather(pre_ffw_gain, "fsdp", axis=0, tiled=True),
        lax.all_gather(post_ffw_gain, "fsdp", axis=0, tiled=True),
        lax.all_gather(query_gain, "fsdp", axis=0, tiled=True),
        lax.all_gather(key_gain, "fsdp", axis=0, tiled=True),
    )
    (
        query_full,
        key_full,
        value_full,
        out_full,
        gate_full,
        up_full,
        down_full,
        gain_attn_in,
        gain_attn_out,
        gain_ffw_in,
        gain_ffw_out,
        gain_query,
        gain_key,
    ) = gathered
    gain_attn_in = gain_attn_in.astype(jnp.float32)
    gain_attn_out = gain_attn_out.astype(jnp.float32)
    gain_ffw_in = gain_ffw_in.astype(jnp.float32)
    gain_ffw_out = gain_ffw_out.astype(jnp.float32)
    gain_query = gain_query.astype(jnp.float32)
    gain_key = gain_key.astype(jnp.float32)
    head_dim = key_full.shape[1]
    head_count = query_full.shape[1] // head_dim
    seq_len = row_count * lax.axis_size("ctx")
    key_span = math.gcd(512, seq_len)
    att_scale = head_dim ** (-0.5)
    flat_rows = seq_count * row_count
    positions = lax.axis_index("ctx") * row_count + jnp.arange(row_count, dtype=jnp.int32)
    x_flat = inputs.astype(jnp.float32).reshape(flat_rows, model_width)
    attn_in, attn_in_back = jax.vjp(norm_gain, x_flat, gain_attn_in)
    attn_in_b = attn_in.astype(jnp.bfloat16)
    query_lin = jnp.dot(attn_in_b, query_full, preferred_element_type=jnp.float32)
    key_lin = jnp.dot(attn_in_b, key_full, preferred_element_type=jnp.float32)
    value_lin = jnp.dot(attn_in_b, value_full, preferred_element_type=jnp.float32)

    def query_side(lin_values, gain_vec):
        return rotate(
            norm_gain(lin_values.reshape(seq_count, row_count, head_count, head_dim), gain_vec),
            positions,
        )

    def key_side(lin_values, gain_vec):
        return rotate(
            norm_gain(lin_values.reshape(seq_count, row_count, 1, head_dim), gain_vec), positions
        )[:, :, 0, :]

    query_rot, query_side_back = jax.vjp(query_side, query_lin, gain_query)
    key_rot, key_side_back = jax.vjp(key_side, key_lin, gain_key)
    query_b = query_rot.astype(jnp.bfloat16)
    key_b = key_rot.astype(jnp.bfloat16)
    value_b = value_lin.reshape(seq_count, row_count, head_dim).astype(jnp.bfloat16)

    def allowed(key_begin, key_count):
        key_pos = key_begin + jnp.arange(key_count, dtype=jnp.int32)
        causal = key_pos[None, :] <= positions[:, None]
        live = key_pos[None, :] < lengths[:, None]
        return (causal[None] & live[:, None, :])[:, None]

    def raw_scores(key_piece):
        return (
            jnp.einsum("sqhd,skd->shqk", query_b, key_piece, preferred_element_type=jnp.float32)
            * att_scale
        )

    stat_shape = (seq_count, head_count, row_count)
    running_max = jnp.full(stat_shape, MASKED_SCORE, jnp.float32)
    key_piece = lax.all_gather(key_b, "ctx", axis=1, tiled=True)
    value_piece = lax.all_gather(value_b, "ctx", axis=1, tiled=True)
    mask_now = allowed(jnp.int32(0), key_piece.shape[1])
    scores = jnp.where(mask_now, raw_scores(key_piece), MASKED_SCORE)
    new_max = jnp.maximum(running_max, jnp.max(scores, axis=-1))
    weights = jnp.where(mask_now, jnp.exp(scores - new_max[..., None]), 0.0)
    new_sum = jnp.sum(weights, axis=-1)
    new_acc = jnp.einsum(
        "shqk,skd->shqd",
        weights.astype(jnp.bfloat16),
        value_piece,
        preferred_element_type=jnp.float32,
    )
    final_state = (new_max, new_sum, new_acc)
    final_max, final_sum, final_acc = final_state
    attended = final_acc / final_sum[..., None]
    log_total = final_max + jnp.log(final_sum)
    attended_b = (
        attended.transpose(0, 2, 1, 3)
        .reshape(flat_rows, head_count * head_dim)
        .astype(jnp.bfloat16)
    )
    attn_lin = jnp.dot(attended_b, out_full, preferred_element_type=jnp.float32)
    attn_post, attn_post_back = jax.vjp(norm_gain, attn_lin, gain_attn_out)
    middle = x_flat + attn_post
    ffw_in, ffw_in_back = jax.vjp(norm_gain, middle, gain_ffw_in)
    ffw_in_b = ffw_in.astype(jnp.bfloat16)
    gate_lin = jnp.dot(ffw_in_b, gate_full, preferred_element_type=jnp.float32)
    up_lin = jnp.dot(ffw_in_b, up_full, preferred_element_type=jnp.float32)
    hidden, hidden_back = jax.vjp(gelu_mix, gate_lin, up_lin)
    hidden_b = hidden.astype(jnp.bfloat16)
    ffw_out = jnp.dot(hidden_b, down_full, preferred_element_type=jnp.float32)
    ffw_post, ffw_post_back = jax.vjp(norm_gain, ffw_out, gain_ffw_out)
    outputs = (middle + ffw_post).astype(jnp.bfloat16).reshape(seq_count, row_count, model_width)
    grad_top = cotangent.astype(jnp.float32).reshape(flat_rows, model_width)
    d_ffw_out, grad_ffw_out_gain = ffw_post_back(grad_top)
    d_ffw_out_b = d_ffw_out.astype(jnp.bfloat16)
    grad_down = jnp.einsum("rf,rd->fd", hidden_b, d_ffw_out_b, preferred_element_type=jnp.float32)
    d_hidden = jnp.einsum("rd,fd->rf", d_ffw_out_b, down_full, preferred_element_type=jnp.float32)
    d_gate, d_up = hidden_back(d_hidden)
    d_gate_b = d_gate.astype(jnp.bfloat16)
    d_up_b = d_up.astype(jnp.bfloat16)
    grad_gate = jnp.einsum("rd,rf->df", ffw_in_b, d_gate_b, preferred_element_type=jnp.float32)
    grad_up = jnp.einsum("rd,rf->df", ffw_in_b, d_up_b, preferred_element_type=jnp.float32)
    d_ffw_in = jnp.einsum(
        "rf,df->rd", d_gate_b, gate_full, preferred_element_type=jnp.float32
    ) + jnp.einsum("rf,df->rd", d_up_b, up_full, preferred_element_type=jnp.float32)
    d_middle_part, grad_ffw_in_gain = ffw_in_back(d_ffw_in)
    d_middle = grad_top + d_middle_part
    d_attn_lin, grad_attn_out_gain = attn_post_back(d_middle)
    d_attn_b = d_attn_lin.astype(jnp.bfloat16)
    grad_projection = jnp.einsum(
        "ro,rd->od", attended_b, d_attn_b, preferred_element_type=jnp.float32
    )
    d_attended_b = (
        jnp.einsum("rd,od->ro", d_attn_b, out_full, preferred_element_type=jnp.float32)
        .astype(jnp.bfloat16)
        .reshape(seq_count, row_count, head_count, head_dim)
    )
    d_attended = d_attended_b.astype(jnp.float32)
    row_delta = jnp.einsum("sqhd,shqd->shq", d_attended, attended, precision=lax.Precision.HIGHEST)

    def key_grads(key_piece, value_piece, key_begin):
        mask_now = allowed(key_begin, key_piece.shape[1])
        probabilities = jnp.where(
            mask_now, jnp.exp(raw_scores(key_piece) - log_total[..., None]), 0.0
        )
        d_probs = jnp.einsum(
            "sqhd,skd->shqk", d_attended_b, value_piece, preferred_element_type=jnp.float32
        )
        d_scores = (probabilities * (d_probs - row_delta[..., None])).astype(jnp.bfloat16)
        d_query = (
            jnp.einsum("shqk,skd->sqhd", d_scores, key_piece, preferred_element_type=jnp.float32)
            * att_scale
        )
        d_key = (
            jnp.einsum("shqk,sqhd->skd", d_scores, query_b, preferred_element_type=jnp.float32)
            * att_scale
        )
        d_value = jnp.einsum(
            "shqk,sqhd->skd",
            probabilities.astype(jnp.bfloat16),
            d_attended_b,
            preferred_element_type=jnp.float32,
        )
        return (d_query, jnp.concatenate([d_key, d_value], axis=-1))

    key_back_all, value_back_all = (
        lax.all_gather(key_b, "ctx", axis=1, tiled=True),
        lax.all_gather(value_b, "ctx", axis=1, tiled=True),
    )

    def slice_keys(key_begin, key_count):
        return (
            lax.dynamic_slice_in_dim(key_back_all, key_begin, key_count, 1),
            lax.dynamic_slice_in_dim(value_back_all, key_begin, key_count, 1),
        )

    query_zero = jnp.zeros((seq_count, row_count, head_count, head_dim), jnp.float32)

    def joint_step(block_id, state):
        d_query_sum, key_buffer = state
        key_begin = block_id * key_span
        key_piece, value_piece = slice_keys(key_begin, key_span)
        d_query, d_keyval = key_grads(key_piece, value_piece, key_begin)
        return (
            d_query_sum + d_query,
            lax.dynamic_update_slice_in_dim(key_buffer, d_keyval, key_begin, 1),
        )

    d_query_rot, key_buffer = lax.fori_loop(
        0,
        seq_len // key_span,
        joint_step,
        (query_zero, jnp.zeros((seq_count, seq_len, 2 * head_dim), jnp.float32)),
    )
    d_keyval_own = lax.psum_scatter(key_buffer, "ctx", scatter_dimension=1, tiled=True)
    d_key_rot = d_keyval_own[..., :head_dim]
    d_value = d_keyval_own[..., head_dim:]
    d_query_lin, grad_query_gain = query_side_back(d_query_rot)
    d_key_lin, grad_key_gain = key_side_back(d_key_rot)
    d_query_b = d_query_lin.astype(jnp.bfloat16)
    d_key_b = d_key_lin.astype(jnp.bfloat16)
    d_value_b = d_value.reshape(flat_rows, head_dim).astype(jnp.bfloat16)
    grad_query = jnp.einsum("rd,rq->dq", attn_in_b, d_query_b, preferred_element_type=jnp.float32)
    grad_key = jnp.einsum("rd,rq->dq", attn_in_b, d_key_b, preferred_element_type=jnp.float32)
    grad_value = jnp.einsum("rd,rq->dq", attn_in_b, d_value_b, preferred_element_type=jnp.float32)
    d_attn_in = jnp.einsum("rq,dq->rd", d_query_b, query_full, preferred_element_type=jnp.float32)
    d_attn_in = d_attn_in + jnp.einsum(
        "rq,dq->rd", d_key_b, key_full, preferred_element_type=jnp.float32
    )
    d_attn_in = d_attn_in + jnp.einsum(
        "rq,dq->rd", d_value_b, value_full, preferred_element_type=jnp.float32
    )
    d_input_part, grad_attn_in_gain = attn_in_back(d_attn_in)
    input_grad = (
        (d_middle + d_input_part).astype(jnp.bfloat16).reshape(seq_count, row_count, model_width)
    )
    shards = (
        lax.psum_scatter(
            grad_query.astype(jnp.bfloat16), "fsdp", scatter_dimension=0, tiled=True
        ).astype(jnp.float32),
        lax.psum_scatter(
            grad_key.astype(jnp.bfloat16), "fsdp", scatter_dimension=0, tiled=True
        ).astype(jnp.float32),
        lax.psum_scatter(
            grad_value.astype(jnp.bfloat16), "fsdp", scatter_dimension=0, tiled=True
        ).astype(jnp.float32),
        lax.psum_scatter(
            grad_projection.astype(jnp.bfloat16), "fsdp", scatter_dimension=0, tiled=True
        ).astype(jnp.float32),
        lax.psum_scatter(
            grad_gate.astype(jnp.bfloat16), "fsdp", scatter_dimension=0, tiled=True
        ).astype(jnp.float32),
        lax.psum_scatter(
            grad_up.astype(jnp.bfloat16), "fsdp", scatter_dimension=0, tiled=True
        ).astype(jnp.float32),
        lax.psum_scatter(
            grad_down.astype(jnp.bfloat16), "fsdp", scatter_dimension=0, tiled=True
        ).astype(jnp.float32),
        lax.psum_scatter(
            grad_attn_in_gain.astype(jnp.bfloat16), "fsdp", scatter_dimension=0, tiled=True
        ).astype(jnp.float32),
        lax.psum_scatter(
            grad_attn_out_gain.astype(jnp.bfloat16), "fsdp", scatter_dimension=0, tiled=True
        ).astype(jnp.float32),
        lax.psum_scatter(
            grad_ffw_in_gain.astype(jnp.bfloat16), "fsdp", scatter_dimension=0, tiled=True
        ).astype(jnp.float32),
        lax.psum_scatter(
            grad_ffw_out_gain.astype(jnp.bfloat16), "fsdp", scatter_dimension=0, tiled=True
        ).astype(jnp.float32),
        lax.psum_scatter(
            grad_query_gain.astype(jnp.bfloat16), "fsdp", scatter_dimension=0, tiled=True
        ).astype(jnp.float32),
        lax.psum_scatter(
            grad_key_gain.astype(jnp.bfloat16), "fsdp", scatter_dimension=0, tiled=True
        ).astype(jnp.float32),
    )
    totals = lax.psum(
        (
            shards[0],
            shards[1],
            shards[2],
            shards[3],
            shards[4],
            shards[5],
            shards[6],
            shards[7],
            shards[8],
            shards[9],
            shards[10],
            shards[11],
            shards[12],
        ),
        "ctx",
    )
    return (outputs, input_grad) + tuple(totals)


def solution(mesh):
    in_specs = (
        P("fsdp", "ctx", None),
        P("fsdp", "ctx", None),
        P("fsdp"),
        P("fsdp", None),
        P("fsdp", None),
        P("fsdp", None),
        P("fsdp", None),
        P("fsdp", None),
        P("fsdp", None),
        P("fsdp", None),
        P("fsdp"),
        P("fsdp"),
        P("fsdp"),
        P("fsdp"),
        P("fsdp"),
        P("fsdp"),
    )
    out_specs = (
        P("fsdp", "ctx", None),
        P("fsdp", "ctx", None),
        P("fsdp", None),
        P("fsdp", None),
        P("fsdp", None),
        P("fsdp", None),
        P("fsdp", None),
        P("fsdp", None),
        P("fsdp", None),
        P("fsdp"),
        P("fsdp"),
        P("fsdp"),
        P("fsdp"),
        P("fsdp"),
        P("fsdp"),
    )
    return jax.shard_map(body, mesh=mesh, in_specs=in_specs, out_specs=out_specs, check_vma=False)
```

profile of v0, /device:TPU:0, one launch (start us, length us, event | category | flops | bytes accessed | tf_op | source)
XLA Modules:
  0.0 893.9 jit_solution(16385621297810421104)
XLA Ops:
  17.0 9.2 %all-reduce.18 = (bf16[256]{0:T(256)(128)(2,1)S(1)}, bf16[640]{0:T(1024)(128)(2,1)S(1)}, bf16[256]{0:T(256)(128)(2,1)S(1)}, bf16[640]{0:T(1024)(128)(2,1)S(1)}, ...) all-reduce(bf16[256]{0:T(256)(128)(2,1)S(1)} %dynamic-update-slice., ...), channel_id=1, replica_groups=mesh['ctx'=8,'fsdp'=4] {'fsdp'}, use_global_device_ids=true, to_apply=%add.5 | all-reduce | flops 3072 | bytes 12288
  26.3 6.2 all_gather.48
  36.3 6.2 all_gather.53
  48.5 2.4 copy.67
  50.9 2.4 multiply_reduce_fusion.3
  58.8 27.3 %all-gather.21.cloned.1.call-done = bf16[4,1024,1,256]{3,1,0,2:T(8,128)(2,1)} async-done(((bf16[4,128,1,256]{3,1,0,2:T(8,128)(2,1)}), bf16[4,1024,1,256]{3,1,0,2:T(8,128)(2,1)}) %all-gather.21.cloned.1.call-update) | async-done | bytes 2097168 | tf_op jit(solution)/shard_map/all_gather | solution.py:141
  86.0 3.3 fusion.28
  89.4 3.2 copy-done.16
  92.7 2.2 fusion.29
  94.9 41.7 %all-gather.11.cloned.1.call-done = bf16[4,1024,256]{2,1,0:T(8,128)(2,1)} async-done(((bf16[4,128,256]{2,1,0:T(8,128)(2,1)}), bf16[4,1024,256]{2,1,0:T(8,128)(2,1)}) %all-gather.11.cloned.1.call-update) | async-done | bytes 2097168 | tf_op jit(solution)/shard_map/all_gather | solution.py:142
  136.6 8.1 fusion.45
  146.8 8.0 all-gather.13.cloned.1.call-done
  154.7 2.8 multiply_reduce_fusion.10
  160.6 21.1 %all-gather.15.cloned.1.call-done = bf16[640,2048]{1,0:T(8,128)(2,1)} async-done(((bf16[160,2048]{1,0:T(8,128)(2,1)}), bf16[640,2048]{1,0:T(8,128)(2,1)}) %all-gather.15.cloned.1.call-update) | async-done | bytes 2621456 | tf_op jit(solution)/shard_map/all_gather | solution.py:65
  181.7 5.8 fusion.78
  187.5 21.2 %all-gather.17.cloned.1.call-done = bf16[640,2048]{1,0:T(8,128)(2,1)} async-done(((bf16[160,2048]{1,0:T(8,128)(2,1)}), bf16[640,2048]{1,0:T(8,128)(2,1)}) %all-gather.17.cloned.1.call-update) | async-done | bytes 2621456 | tf_op jit(solution)/shard_map/all_gather | solution.py:66
  208.7 8.3 multiply_convert_fusion.1
  217.0 18.9 %all-gather.19.cloned.1.call-done = bf16[2048,640]{1,0:T(8,128)(2,1)} async-done(((bf16[512,640]{1,0:T(8,128)(2,1)}), bf16[2048,640]{1,0:T(8,128)(2,1)}) %all-gather.19.cloned.1.call-update) | async-done | bytes 2621456 | tf_op jit(solution)/shard_map/all_gather | solution.py:67
  235.9 4.4 multiply_reduce_fusion.8
  243.6 4.8 multiply_convert_fusion
  251.7 2.1 multiply_reduce_fusion.4
  258.7 3.5 convolution_convert_fusion.5
  262.2 2.6 reshape.457
  264.8 2.4 copy.71
  267.2 2.9 bitcast_convert_fusion
  270.3 3.0 multiply_reduce_fusion
  273.3 4.3 broadcast_in_dim.140.clone
  277.6 40.3 %while.16 = (s32[]{:T(128)}, f32[4,128,4,256]{1,3,2,0:T(8,128)S(1)}, f32[4,1024,512]{2,1,0:T(8,128)}, bf16[4,1024,256]{2,1,0:T(8,128)(2,1)}, s32[4]{0:T(128)S(1)...) while((s32[]{:T(128)}, ...), condition=%wide.region_12.13_spmd.clone, body=%wide.region_11.12_spmd.clone.sunk | while | flops 2698316288 | bytes 81694016 | solution.py:251
  285.7 2.4 pad_maximum_fusion.5
  288.1 5.3 copy.128
  293.4 4.6 constant_dynamic-update-slice_fusion.2
  305.6 2.4 pad_maximum_fusion.5
  308.0 5.3 copy.128
  313.3 4.6 constant_dynamic-update-slice_fusion.2
  327.6 4.6 convolution_convert_fusion.2
  332.5 4.8 convolution_convert_fusion.1
  338.3 4.9 convolution_convert_fusion
  345.4 3.3 fusion.80
  348.7 5.6 reduce-scatter.11.cloned.1.call-done
  354.4 37.1 %reduce-scatter.19.cloned.1.call-done = bf16[160,2048]{1,0:T(8,128)(2,1)} async-done(((bf16[640,2048]{1,0:T(8,128)(2,1)}), bf16[160,2048]{1,0:T(8,128)(2,1)}) %reduce-scatter.19.cloned.1.call-update) | async-done | bytes 655376 | tf_op jit(solution)/shard_map/reduce_scatter | solution.py:292
  391.5 37.4 %reduce-scatter.21.cloned.1.call-done = bf16[160,2048]{1,0:T(8,128)(2,1)} async-done(((bf16[640,2048]{1,0:T(8,128)(2,1)}), bf16[160,2048]{1,0:T(8,128)(2,1)}) %reduce-scatter.21.cloned.1.call-update) | async-done | bytes 655376 | tf_op jit(solution)/shard_map/reduce_scatter | solution.py:295
  428.9 37.1 %reduce-scatter.23.cloned.1.call-done = bf16[512,640]{1,0:T(8,128)(2,1)} async-done(((bf16[2048,640]{1,0:T(8,128)(2,1)}), bf16[512,640]{1,0:T(8,128)(2,1)}) %reduce-scatter.23.cloned.1.call-update) | async-done | bytes 655376 | tf_op jit(solution)/shard_map/reduce_scatter | solution.py:298
  466.0 153.5 %reduce-scatter.9.cloned.1.call-done = f32[4,128,512]{2,1,0:T(8,128)} async-done(((f32[4,1024,512]{2,1,0:T(8,128)}), f32[4,128,512]{2,1,0:T(8,128)}) %reduce-scatter.9.cloned.1.call-update) | async-done | bytes 1048592 | tf_op jit(solution)/shard_map/reduce_scatter | solution.py:257
  627.2 7.1 all-reduce.17
  635.9 2.7 fusion.52
  638.6 3.3 reduce-scatter.15.cloned.1.call-done
  641.9 23.6 %reduce-scatter.13.cloned.1.call-done = bf16[160,256]{1,0:T(8,128)(2,1)} async-done(((bf16[640,256]{1,0:T(8,128)(2,1)}), bf16[160,256]{1,0:T(8,128)(2,1)}) %reduce-scatter.13.cloned.1.call-update) | async-done | bytes 81936 | tf_op jit(solution)/shard_map/reduce_scatter | solution.py:283
  665.5 221.7 %all-reduce.20 = (f32[160,1024]{1,0:T(8,128)}, f32[160,256]{1,0:T(8,128)}, f32[160,256]{1,0:T(8,128)}, f32[256,640]{1,0:T(8,128)}, f32[160,2048]{1,0:T(8,128)}, ...) all-reduce(bf16[160,1024]{1,0:T(8,128)(2,1)} %reduce-scatter.11.clo, ...), channel_id=1, replica_groups=mesh['ctx'=8,'fsdp'=4] {'ctx'}, use_global_device_ids=true, to_apply=%region_18.19 | all-reduce | flops 1393408 | bytes 8361984 | tf_op jit(solution)/shard_map/psum | solution.py:320
  (278 shorter events, 75.7 us)
Async XLA Ops:
  7.2 41.3 %all-gather.9.cloned.1.call-start = ((), (), s32[]{:S(2)}) async-start(), calls=%async_computation.8 | async-start | bytes 1638400 | tf_op jit(solution)/shard_map/all_gather | solution.py:61
  7.9 78.1 %all-gather.21.cloned.1.call-start = ((), (), s32[]{:S(2)}) async-start(), calls=%async_computation.22 | async-start | bytes 2359296 | tf_op jit(solution)/shard_map/all_gather | solution.py:141
  11.9 30.6 %copy-start.51 = (f32[4,128]{1,0:T(4,128)}, f32[4,128]{1,0:T(4,128)S(1)}, u32[]{:S(2)}) copy-start(f32[4,128]{1,0:T(4,128)S(1)} %fusion.58) | copy-start | bytes 6148
  11.9 20.5 %copy-start.47 = (f32[512]{0:T(512)}, f32[512]{0:T(512)S(1)}, u32[]{:S(2)}) copy-start(f32[512]{0:T(512)S(1)} %bitcast_rsqrt_fusion.1) | copy-start | bytes 6148
  26.2 9.1 %copy-start.56 = (f32[256]{0:T(256)}, f32[256]{0:T(256)S(1)}, u32[]{:S(2)}) copy-start(f32[256]{0:T(256)S(1)} %convert_add_fusion.6) | copy-start | bytes 3076
  32.4 3.0 copy-start.20
  32.4 10.0 %copy-start.42 = (f32[640]{0:T(1024)}, f32[640]{0:T(1024)S(1)}, u32[]{:S(2)}) copy-start(f32[640]{0:T(1024)S(1)} %convert_add_fusion.4) | copy-start | bytes 7684
  33.9 2.4 copy-start.44
  33.9 8.6 copy-start.3
  34.7 19.6 %copy-start.25 = (f32[128,128]{1,0:T(8,128)}, f32[128,128]{1,0:T(8,128)S(1)}, u32[]{:S(2)}) copy-start(f32[128,128]{1,0:T(8,128)S(1)} %get-tuple-element.348) | copy-start | bytes 196612
  34.7 19.6 %copy-start.27 = (f32[128,128]{1,0:T(8,128)}, f32[128,128]{1,0:T(8,128)S(1)}, u32[]{:S(2)}) copy-start(f32[128,128]{1,0:T(8,128)S(1)} %get-tuple-element.349) | copy-start | bytes 196612
  36.2 100.4 %all-gather.11.cloned.1.call-start = ((), (), s32[]{:S(2)}) async-start(), calls=%async_computation.9 | async-start | bytes 2359296 | tf_op jit(solution)/shard_map/all_gather | solution.py:142
  42.5 3.1 copy-start.18
  42.7 8.2 copy-start.14
  42.7 3.7 copy-start.55
  43.9 110.9 %all-gather.13.cloned.1.call-start = ((), (), s32[]{:S(2)}) async-start(), calls=%async_computation.10 | async-start | bytes 1638400 | tf_op jit(solution)/shard_map/all_gather | solution.py:64
  44.4 137.3 %all-gather.15.cloned.1.call-start = ((), (), s32[]{:S(2)}) async-start(), calls=%async_computation.11 | async-start | bytes 3276800 | tf_op jit(solution)/shard_map/all_gather | solution.py:65
  45.0 163.7 %all-gather.17.cloned.1.call-start = ((), (), s32[]{:S(2)}) async-start(), calls=%async_computation.12 | async-start | bytes 3276800 | tf_op jit(solution)/shard_map/all_gather | solution.py:66
  45.6 190.3 %all-gather.19.cloned.1.call-start = ((), (), s32[]{:S(2)}) async-start(), calls=%async_computation.13 | async-start | bytes 3276800 | tf_op jit(solution)/shard_map/all_gather | solution.py:67
  46.4 302.3 %reduce-scatter.17.cloned.1.call-start = ((), (), s32[]{:S(2)}) async-start(), calls=%async_computation.18 | async-start | bytes 1638400 | tf_op jit(solution)/shard_map/reduce_scatter | solution.py:289
  46.4 7.5 copy-start.58
  86.0 6.6 copy-start.22
  89.4 3.3 copy-start.16
  154.7 2.8 copy-start.4
  235.9 4.4 copy-start.17
  235.9 7.1 copy-start.64
  235.9 7.1 copy-start.67
  243.0 5.4 copy-start.34
  243.6 4.9 copy-start.60
  248.5 3.2 copy-start.61
  270.2 84.1 %reduce-scatter.11.cloned.1.call-start = ((), (), s32[]{:S(2)}) async-start(), calls=%async_computation.15 | async-start | bytes 1638400 | tf_op jit(solution)/shard_map/reduce_scatter | solution.py:280
  327.6 63.9 %reduce-scatter.19.cloned.1.call-start = ((), (), s32[]{:S(2)}) async-start(), calls=%async_computation.19 | async-start | bytes 3276800 | tf_op jit(solution)/shard_map/reduce_scatter | solution.py:292
  332.3 96.6 %reduce-scatter.21.cloned.1.call-start = ((), (), s32[]{:S(2)}) async-start(), calls=%async_computation.20 | async-start | bytes 3276800 | tf_op jit(solution)/shard_map/reduce_scatter | solution.py:295
  337.3 128.8 %reduce-scatter.23.cloned.1.call-start = ((), (), s32[]{:S(2)}) async-start(), calls=%async_computation.21 | async-start | bytes 3276800 | tf_op jit(solution)/shard_map/reduce_scatter | solution.py:298
  343.3 276.2 %reduce-scatter.9.cloned.1.call-start = ((), (), s32[]{:S(2)}) async-start(), calls=%async_computation.14 | async-start | bytes 9437184 | tf_op jit(solution)/shard_map/reduce_scatter | solution.py:257
  344.0 297.9 %reduce-scatter.15.cloned.1.call-start = ((), (), s32[]{:S(2)}) async-start(), calls=%async_computation.17 | async-start | bytes 409600 | tf_op jit(solution)/shard_map/reduce_scatter | solution.py:286
  348.7 273.4 %copy-start.9 = (f32[512,256]{1,0:T(8,128)S(1)}, f32[512,256]{1,0:T(8,128)}, u32[]{:S(2)}) copy-start(f32[512,256]{1,0:T(8,128)} %copy-done.8) | copy-start | bytes 1572868
  348.7 273.4 %copy-start.50 = (f32[4,128]{1,0:T(4,128)S(1)}, f32[4,128]{1,0:T(4,128)}, u32[]{:S(2)}) copy-start(f32[4,128]{1,0:T(4,128)} %copy-done.49) | copy-start | bytes 6148
  348.7 273.4 %copy-start.57 = (f32[256]{0:T(256)S(1)}, f32[256]{0:T(256)}, u32[]{:S(2)}) copy-start(f32[256]{0:T(256)} %copy-done.56) | copy-start | bytes 3076
  622.0 43.4 %reduce-scatter.13.cloned.1.call-start = ((), (), s32[]{:S(2)}) async-start(), calls=%async_computation.16 | async-start | bytes 409600 | tf_op jit(solution)/shard_map/reduce_scatter | solution.py:283
  622.6 2.9 copy-start.5
  622.6 2.9 copy-start.19
  622.6 2.9 copy-start.43
  622.6 2.9 copy-start.48
  625.6 10.4 %copy-start.52 = (f32[4,128]{1,0:T(4,128)S(1)}, f32[4,128]{1,0:T(4,128)}, u32[]{:S(2)}) copy-start(f32[4,128]{1,0:T(4,128)} %copy-done.51) | copy-start | bytes 6148
  625.6 10.4 %copy-start.13 = (f32[512,640]{1,0:T(8,128)S(1)}, f32[512,640]{1,0:T(8,128)}, u32[]{:S(2)}) copy-start(f32[512,640]{1,0:T(8,128)} %copy-done.12) | copy-start | bytes 3932164
  635.7 29.7 %copy-start.36 = (bf16[160,2048]{1,0:T(8,128)(2,1)S(1)}, bf16[160,2048]{1,0:T(8,128)(2,1)}, u32[]{:S(2)}) copy-start(bf16[160,2048]{1,0:T(8,128)(2,1)} %reduce-scatter.19.cloned.1.call-done) | copy-start | bytes 1966084
  635.7 29.7 %copy-start.37 = (bf16[160,2048]{1,0:T(8,128)(2,1)S(1)}, bf16[160,2048]{1,0:T(8,128)(2,1)}, u32[]{:S(2)}) copy-start(bf16[160,2048]{1,0:T(8,128)(2,1)} %reduce-scatter.21.cloned.1.call-done) | copy-start | bytes 1966084
  (38 other events, 60.4 us)
Sparse Core Ops, SparseCore 0:
  9.6 21.7 all-gather.8
  36.3 49.7 all-gather.20
  88.8 47.7 all-gather.10
  138.0 16.6 all-gather.12
  156.1 25.5 all-gather.14
  183.1 25.5 all-gather.16
  210.3 25.5 all-gather.18
  270.3 26.5 reduce-scatter.16
  327.7 26.6 reduce-scatter.10
  356.7 34.6 reduce-scatter.18
  394.2 34.6 reduce-scatter.20
  431.3 34.6 reduce-scatter.22
  470.1 149.3 reduce-scatter.8
  622.4 19.4 reduce-scatter.14
  645.0 20.4 reduce-scatter.12
where the time goes:
time: 902 us; the launch traced here: 894 us
  waiting for transfers between devices  440 us (49%)
  blocking collectives  250 us (28%)
  matrix products  88.8 us (10%)
  local copies, waits for them, and re-layouts  62.2 us (7%)
  other arithmetic  33.9 us (4%)
  between operations  17.6 us (2%)
    psum x1, blocking collectives, body(): lax.psum((shards[0], shards[1], shards[2], shards[3], shards[4], shards[5...  222 us
    reduce_scatter x1, waiting for transfers between devices, body(): lax.psum_scatter(key_buffer, 'ctx', scatter_dimension=1, tiled=True)  153 us
    all_gather x1, waiting for transfers between devices, body(): value_piece = lax.all_gather(value_b, 'ctx', axis=1, tiled=True)  41.7 us
    reduce_scatter x1, waiting for transfers between devices, body(): lax.psum_scatter(grad_up.astype(jnp.bfloat16), 'fsdp', scatter_dimension=...  37.4 us
    reduce_scatter x1, waiting for transfers between devices, body(): lax.psum_scatter(grad_down.astype(jnp.bfloat16), 'fsdp', scatter_dimensio...  37.1 us
    reduce_scatter x1, waiting for transfers between devices, body(): lax.psum_scatter(grad_gate.astype(jnp.bfloat16), 'fsdp', scatter_dimensio...  37.1 us
    all_gather x1, waiting for transfers between devices, body(): key_piece = lax.all_gather(key_b, 'ctx', axis=1, tiled=True)  27.3 us
    unnamed x147, local copies, waits for them, and re-layouts  25.9 us
  transfers between devices with their start and end apart: 15, of which 13 were waited for; matrix products, arithmetic and copies ran while one was open for 15% of the time, Pallas kernels for 0%

commit v1 on v0

--- a/solution.py
+++ b/solution.py
@@ -7,6 +7,17 @@
 EPSILON = 1e-06
 MASKED_SCORE = -1e30
 ROPE_BASE = 1000000.0
+
+
+def turned_line(x, axis, dim):
+    size = lax.axis_size(axis)
+    route = [(i, (i + 1) % size) for i in range(size)]
+    pieces = [x]
+    for far in range(1, size):
+        pieces = [lax.ppermute(pieces[0], axis, route), *pieces]
+    whole = jnp.concatenate(pieces, axis=dim)
+    turn = (lax.axis_index(axis) + 1) * pieces[-1].shape[dim]
+    return jnp.roll(whole, turn, axis=dim)
 
 
 def norm_gain(values, gain_vec):
@@ -138,7 +149,7 @@
 
     stat_shape = (seq_count, head_count, row_count)
     running_max = jnp.full(stat_shape, MASKED_SCORE, jnp.float32)
-    key_piece = lax.all_gather(key_b, "ctx", axis=1, tiled=True)
+    key_piece = turned_line(key_b, "ctx", 1)
     value_piece = lax.all_gather(value_b, "ctx", axis=1, tiled=True)
     mask_now = allowed(jnp.int32(0), key_piece.shape[1])
     scores = jnp.where(mask_now, raw_scores(key_piece), MASKED_SCORE)

time: 902 us -> 877 us (0.972)
  waiting for transfers between devices: 440 us -> 394 us
  local copies, waits for them, and re-layouts: 62.2 us -> 75.8 us
    ppermute x0 -> x7, waiting for transfers between devices: none -> 79 us  [turned_line(): pieces = [lax.ppermute(pieces[0], axis, route), *pieces]]
    all_gather x1, waiting for transfers between devices: 41.7 us -> 0.02 us  [body(): value_piece = lax.all_gather(value_b, 'ctx', axis=1, tiled=True)]
    all_gather x1, waiting for transfers between devices: 21.2 us -> 0.01 us  [body(): lax.all_gather(up_weight, 'fsdp', axis=0, tiled=True)]
    all_gather x1, waiting for transfers between devices: 21.1 us -> 0.01 us  [body(): lax.all_gather(gate_weight, 'fsdp', axis=0, tiled=True)]
    all_gather x1, waiting for transfers between devices: 18.9 us -> 1.2 us  [body(): lax.all_gather(down_weight, 'fsdp', axis=0, tiled=True)]
    unnamed x147 -> x177, local copies, waits for them, and re-layouts: 25.9 us -> 39.4 us
    all_gather x1, waiting for transfers between devices: 27.3 us -> 14.1 us  [body(): lax.all_gather(key_b, 'ctx', axis=1, tiled=True)]
  transfers between devices with their start and end apart: 15 -> 22, of which waited for: 13 -> 16; matrix products, arithmetic and copies ran while one was open for 15% -> 21% of each run, Pallas kernels for 0% -> 0%
where the time goes in v1:
time: 877 us; the launch traced here: 868 us
  waiting for transfers between devices  394 us (45%)
  blocking collectives  251 us (29%)
  matrix products  89.3 us (10%)
  local copies, waits for them, and re-layouts  75.8 us (9%)
  other arithmetic  37.2 us (4%)
  between operations  17.7 us (2%)
    psum x1, blocking collectives, body(): lax.psum((shards[0], shards[1], shards[2], shards[3], shards[4], shards[5...  222 us
    reduce_scatter x1, waiting for transfers between devices, body(): lax.psum_scatter(key_buffer, 'ctx', scatter_dimension=1, tiled=True)  154 us
    ppermute x7, waiting for transfers between devices, turned_line(): pieces = [lax.ppermute(pieces[0], axis, route), *pieces]  79 us
    unnamed x177, local copies, waits for them, and re-layouts  39.4 us
    reduce_scatter x1, waiting for transfers between devices, body(): lax.psum_scatter(grad_up.astype(jnp.bfloat16), 'fsdp', scatter_dimension=...  37.4 us
    reduce_scatter x1, waiting for transfers between devices, body(): lax.psum_scatter(grad_down.astype(jnp.bfloat16), 'fsdp', scatter_dimensio...  37.1 us
    reduce_scatter x1, waiting for transfers between devices, body(): lax.psum_scatter(grad_gate.astype(jnp.bfloat16), 'fsdp', scatter_dimensio...  37.1 us
    reduce_scatter x1, waiting for transfers between devices, body(): lax.psum_scatter(grad_key.astype(jnp.bfloat16), 'fsdp', scatter_dimension...  23.5 us
  transfers between devices with their start and end apart: 22, of which 16 were waited for; matrix products, arithmetic and copies ran while one was open for 21% of the time, Pallas kernels for 0%

profile of v1, /device:TPU:0, one launch (start us, length us, event | category | flops | bytes accessed | tf_op | source)
XLA Modules:
  0.0 868.0 jit_solution(13763990951155789459)
XLA Ops:
  15.7 9.0 %all-reduce.18 = (bf16[256]{0:T(256)(128)(2,1)S(1)}, bf16[640]{0:T(1024)(128)(2,1)S(1)}, bf16[256]{0:T(256)(128)(2,1)S(1)}, bf16[640]{0:T(1024)(128)(2,1)S(1)}, ...) all-reduce(bf16[256]{0:T(256)(128)(2,1)S(1)} %dynamic-update-slice., ...), channel_id=1, replica_groups=mesh['ctx'=8,'fsdp'=4] {'fsdp'}, use_global_device_ids=true, to_apply=%add.5 | all-reduce | flops 3072 | bytes 12288
  24.7 7.1 all_gather.51
  38.2 6.2 all_gather.47
  48.5 15.2 %collective-permute-done = bf16[4,128,256]{2,1,0:T(8,128)(2,1)S(1)} collective-permute-done((bf16[4,128,256]{2,1,0:T(8,128)(2,1)S(1)}, bf16[4,128,256]{2,1,0:T(8,128)(2,1)S(1)}, u32[]{:S(2)}, u32[]{:S(2)}) %collective-permute-start) | collective-permute-done | bytes 262176 | tf_op jit(solution)/shard_map/ppermute | solution.py:17
  63.7 14.9 %collective-permute-done.1 = bf16[4,128,256]{2,1,0:T(8,128)(2,1)S(1)} collective-permute-done((bf16[4,128,256]{2,1,0:T(8,128)(2,1)S(1)}, bf16[4,128,256]{2,1,0:T(8,128)(2,1)S(1)}, u32[]{:S(2)}, u32[]{:S(2)}) %collective-permute-start.1) | collective-permute-done | bytes 262176 | tf_op jit(solution)/shard_map/ppermute | solution.py:17
  79.3 15.6 %collective-permute-done.2 = bf16[4,128,256]{2,1,0:T(8,128)(2,1)S(1)} collective-permute-done((bf16[4,128,256]{2,1,0:T(8,128)(2,1)S(1)}, bf16[4,128,256]{2,1,0:T(8,128)(2,1)S(1)}, u32[]{:S(2)}, u32[]{:S(2)}) %collective-permute-start.2) | collective-permute-done | bytes 262176 | tf_op jit(solution)/shard_map/ppermute | solution.py:17
  95.0 9.0 %collective-permute-done.3 = bf16[4,128,256]{2,1,0:T(8,128)(2,1)S(1)} collective-permute-done((bf16[4,128,256]{2,1,0:T(8,128)(2,1)S(1)}, bf16[4,128,256]{2,1,0:T(8,128)(2,1)S(1)}, u32[]{:S(2)}, u32[]{:S(2)}) %collective-permute-start.3) | collective-permute-done | bytes 262176 | tf_op jit(solution)/shard_map/ppermute | solution.py:17
  104.0 9.0 %collective-permute-done.4 = bf16[4,128,256]{2,1,0:T(8,128)(2,1)S(1)} collective-permute-done((bf16[4,128,256]{2,1,0:T(8,128)(2,1)S(1)}, bf16[4,128,256]{2,1,0:T(8,128)(2,1)S(1)}, u32[]{:S(2)}, u32[]{:S(2)}) %collective-permute-start.4) | collective-permute-done | bytes 262176 | tf_op jit(solution)/shard_map/ppermute | solution.py:17
  113.8 9.2 %collective-permute-done.5 = bf16[4,128,256]{2,1,0:T(8,128)(2,1)} collective-permute-done((bf16[4,128,256]{2,1,0:T(8,128)(2,1)S(1)}, bf16[4,128,256]{2,1,0:T(8,128)(2,1)}, u32[]{:S(2)}, u32[]{:S(2)}) %collective-permute-start.5) | collective-permute-done | bytes 262176 | tf_op jit(solution)/shard_map/ppermute | solution.py:17
  123.6 2.6 broadcast_and_fusion.1
  126.3 6.1 collective-permute-done.6
  148.9 2.4 copy.67
  151.3 2.5 multiply_reduce_fusion.3
  159.2 3.4 fusion.28
  165.9 8.2 fusion.45
  176.1 2.8 multiply_reduce_fusion.10
  182.1 5.7 fusion.81
  187.8 8.3 multiply_convert_fusion.1
  197.3 4.4 multiply_reduce_fusion.8
  205.0 4.8 multiply_convert_fusion
  220.0 2.6 reshape.457
  222.7 2.4 copy.71
  225.1 3.7 convolution_convert_fusion.3
  228.7 2.8 bitcast_convert_fusion
  231.7 3.0 multiply_reduce_fusion
  234.7 14.1 %all-gather.21.cloned.1.call-done = bf16[4,1024,1,256]{3,1,0,2:T(8,128)(2,1)} async-done(((bf16[4,128,1,256]{3,1,0,2:T(8,128)(2,1)}), bf16[4,1024,1,256]{3,1,0,2:T(8,128)(2,1)}) %all-gather.21.cloned.1.call-update) | async-done | bytes 2097168 | tf_op jit(solution)/shard_map/all_gather | solution.py:240
  248.8 4.4 broadcast_in_dim.140.clone
  253.2 40.5 %while.16 = (s32[]{:T(128)}, f32[4,128,4,256]{1,3,2,0:T(8,128)S(1)}, f32[4,1024,512]{2,1,0:T(8,128)}, bf16[4,1024,256]{2,1,0:T(8,128)(2,1)}, s32[4]{0:T(128)S(1)...) while((s32[]{:T(128)}, ...), condition=%wide.region_12.13_spmd.clone, body=%wide.region_11.12_spmd.clone.sunk | while | flops 2698316288 | bytes 81694016 | solution.py:262
  261.4 2.4 pad_maximum_fusion.5
  263.8 5.3 copy.128
  269.1 4.6 constant_dynamic-update-slice_fusion.18
  281.3 2.4 pad_maximum_fusion.5
  283.7 5.3 copy.128
  289.0 4.7 constant_dynamic-update-slice_fusion.18
  303.3 4.6 convolution_convert_fusion.2
  308.2 4.9 convolution_convert_fusion.1
  314.1 4.9 convolution_convert_fusion
  321.2 3.3 fusion.83
  324.5 4.0 reduce-scatter.11.cloned.1.call-done
  328.5 37.1 %reduce-scatter.19.cloned.1.call-done = bf16[160,2048]{1,0:T(8,128)(2,1)} async-done(((bf16[640,2048]{1,0:T(8,128)(2,1)}), bf16[160,2048]{1,0:T(8,128)(2,1)}) %reduce-scatter.19.cloned.1.call-update) | async-done | bytes 655376 | tf_op jit(solution)/shard_map/reduce_scatter | solution.py:303
  365.6 37.4 %reduce-scatter.21.cloned.1.call-done = bf16[160,2048]{1,0:T(8,128)(2,1)} async-done(((bf16[640,2048]{1,0:T(8,128)(2,1)}), bf16[160,2048]{1,0:T(8,128)(2,1)}) %reduce-scatter.21.cloned.1.call-update) | async-done | bytes 655376 | tf_op jit(solution)/shard_map/reduce_scatter | solution.py:306
  403.0 37.1 %reduce-scatter.23.cloned.1.call-done = bf16[512,640]{1,0:T(8,128)(2,1)} async-done(((bf16[2048,640]{1,0:T(8,128)(2,1)}), bf16[512,640]{1,0:T(8,128)(2,1)}) %reduce-scatter.23.cloned.1.call-update) | async-done | bytes 655376 | tf_op jit(solution)/shard_map/reduce_scatter | solution.py:309
  440.1 153.5 %reduce-scatter.9.cloned.1.call-done = f32[4,128,512]{2,1,0:T(8,128)} async-done(((f32[4,1024,512]{2,1,0:T(8,128)}), f32[4,128,512]{2,1,0:T(8,128)}) %reduce-scatter.9.cloned.1.call-update) | async-done | bytes 1048592 | tf_op jit(solution)/shard_map/reduce_scatter | solution.py:268
  601.4 7.1 all-reduce.17
  610.1 2.7 fusion.53
  612.7 3.3 reduce-scatter.15.cloned.1.call-done
  616.0 23.5 %reduce-scatter.13.cloned.1.call-done = bf16[160,256]{1,0:T(8,128)(2,1)} async-done(((bf16[640,256]{1,0:T(8,128)(2,1)}), bf16[160,256]{1,0:T(8,128)(2,1)}) %reduce-scatter.13.cloned.1.call-update) | async-done | bytes 81936 | tf_op jit(solution)/shard_map/reduce_scatter | solution.py:294
  639.6 221.7 %all-reduce.20 = (f32[160,1024]{1,0:T(8,128)}, f32[160,256]{1,0:T(8,128)}, f32[160,256]{1,0:T(8,128)}, f32[256,640]{1,0:T(8,128)}, f32[160,2048]{1,0:T(8,128)}, ...) all-reduce(bf16[160,1024]{1,0:T(8,128)(2,1)} %reduce-scatter.11.clo, ...), channel_id=1, replica_groups=mesh['ctx'=8,'fsdp'=4] {'ctx'}, use_global_device_ids=true, to_apply=%region_18.19 | all-reduce | flops 1393408 | bytes 8361984 | tf_op jit(solution)/shard_map/psum | solution.py:331
  (324 shorter events, 100.3 us)
Async XLA Ops:
  7.2 141.7 %all-gather.9.cloned.1.call-start = ((), (), s32[]{:S(2)}) async-start(), calls=%async_computation.8 | async-start | bytes 1638400 | tf_op jit(solution)/shard_map/all_gather | solution.py:72
  7.9 158.0 %all-gather.11.cloned.1.call-start = ((), (), s32[]{:S(2)}) async-start(), calls=%async_computation.9 | async-start | bytes 2359296 | tf_op jit(solution)/shard_map/all_gather | solution.py:153
  33.1 11.3 %copy-start.58 = (f32[4,128]{1,0:T(4,128)}, f32[4,128]{1,0:T(4,128)S(1)}, u32[]{:S(2)}) copy-start(f32[4,128]{1,0:T(4,128)S(1)} %fusion.59) | copy-start | bytes 6148
  33.2 11.3 %copy-start.49 = (f32[640]{0:T(1024)}, f32[640]{0:T(1024)S(1)}, u32[]{:S(2)}) copy-start(f32[640]{0:T(1024)S(1)} %convert_add_fusion.4) | copy-start | bytes 7684
  34.5 116.8 %copy-start.14 = (bf16[4,128,640]{2,1,0:T(8,128)(2,1)}, bf16[4,128,640]{2,1,0:T(8,128)(2,1)S(1)}, u32[]{:S(2)}) copy-start(bf16[4,128,640]{2,1,0:T(8,128)(2,1)S(1)} %fusion.61) | copy-start | bytes 1966084
  34.5 10.0 %copy-start.3 = (bf16[4,128,640]{2,1,0:T(8,128)(2,1)S(1)}, bf16[4,128,640]{2,1,0:T(8,128)(2,1)}, u32[]{:S(2)}) copy-start(bf16[4,128,640]{2,1,0:T(8,128)(2,1)} %param.18) | copy-start | bytes 1966084
  35.6 140.4 %all-gather.13.cloned.1.call-start = ((), (), s32[]{:S(2)}) async-start(), calls=%async_computation.10 | async-start | bytes 1638400 | tf_op jit(solution)/shard_map/all_gather | solution.py:75
  36.4 145.7 %all-gather.15.cloned.1.call-start = ((), (), s32[]{:S(2)}) async-start(), calls=%async_computation.11 | async-start | bytes 3276800 | tf_op jit(solution)/shard_map/all_gather | solution.py:76
  37.0 150.8 %all-gather.17.cloned.1.call-start = ((), (), s32[]{:S(2)}) async-start(), calls=%async_computation.12 | async-start | bytes 3276800 | tf_op jit(solution)/shard_map/all_gather | solution.py:77
  37.6 159.8 %all-gather.19.cloned.1.call-start = ((), (), s32[]{:S(2)}) async-start(), calls=%async_computation.13 | async-start | bytes 3276800 | tf_op jit(solution)/shard_map/all_gather | solution.py:78
  38.1 210.7 %all-gather.21.cloned.1.call-start = ((), (), s32[]{:S(2)}) async-start(), calls=%async_computation.22 | async-start | bytes 2359296 | tf_op jit(solution)/shard_map/all_gather | solution.py:240
  44.7 68.3 %copy-start.62 = (s32[4]{0:T(128)S(1)}, s32[4]{0:T(128)}, u32[]{:S(2)}) copy-start(s32[4]{0:T(128)} %param.20) | copy-start | bytes 52
  45.2 78.3 %copy-start.60 = (f32[512]{0:T(512)}, f32[512]{0:T(512)S(1)}, u32[]{:S(2)}) copy-start(f32[512]{0:T(512)S(1)} %get-tuple-element.354) | copy-start | bytes 6148
  45.2 78.3 %copy-start.56 = (f32[4,128]{1,0:T(4,128)}, f32[4,128]{1,0:T(4,128)S(1)}, u32[]{:S(2)}) copy-start(f32[4,128]{1,0:T(4,128)S(1)} %bitcast_rsqrt_fusion) | copy-start | bytes 6148
  45.6 108.7 %copy-start.25 = (f32[128,128]{1,0:T(8,128)}, f32[128,128]{1,0:T(8,128)S(1)}, u32[]{:S(2)}) copy-start(f32[128,128]{1,0:T(8,128)S(1)} %get-tuple-element.350) | copy-start | bytes 196612
  45.6 108.7 %copy-start.27 = (f32[128,128]{1,0:T(8,128)}, f32[128,128]{1,0:T(8,128)S(1)}, u32[]{:S(2)}) copy-start(f32[128,128]{1,0:T(8,128)S(1)} %get-tuple-element.351) | copy-start | bytes 196612
  47.0 16.7 %collective-permute-start = (bf16[4,128,256]{2,1,0:T(8,128)(2,1)S(1)}, bf16[4,128,256]{2,1,0:T(8,128)(2,1)S(1)}, u32[]{:S(2)}, u32[]{:S(2)}) collective-permute-start(bf16[4,128,256]{2,1,0:T(8,128)(2,1)S(1)} %get-tuple-element.349), channel_id=1, source_target_pairs={{0,4},{4,8},{8,12},{12,16},{16,20},{20,24},{24,28},{28,0},{1,5},{5... | collective-permute-start | bytes 786440 | tf_op jit(solution)/shard_map/ppermute | solution.py:17
  63.7 14.9 %collective-permute-start.1 = (bf16[4,128,256]{2,1,0:T(8,128)(2,1)S(1)}, bf16[4,128,256]{2,1,0:T(8,128)(2,1)S(1)}, u32[]{:S(2)}, u32[]{:S(2)}) collective-permute-start(bf16[4,128,256]{2,1,0:T(8,128)(2,1)S(1)} %collective-permute-done), channel_id=1, source_target_pairs={{0,4},{4,8},{8,12},{12,16},{16,20},{20,24},{24,28},{28,0},{1,5},{5... | collective-permute-start | bytes 786440 | tf_op jit(solution)/shard_map/ppermute | solution.py:17
  79.3 15.6 %collective-permute-start.2 = (bf16[4,128,256]{2,1,0:T(8,128)(2,1)S(1)}, bf16[4,128,256]{2,1,0:T(8,128)(2,1)S(1)}, u32[]{:S(2)}, u32[]{:S(2)}) collective-permute-start(bf16[4,128,256]{2,1,0:T(8,128)(2,1)S(1)} %collective-permute-done.1), channel_id=1, source_target_pairs={{0,4},{4,8},{8,12},{12,16},{16,20},{20,24},{24,28},{28,0},{1,5},{5... | collective-permute-start | bytes 786440 | tf_op jit(solution)/shard_map/ppermute | solution.py:17
  94.9 28.7 %copy-start.35 = (bf16[4,128,256]{2,1,0:T(8,128)(2,1)}, bf16[4,128,256]{2,1,0:T(8,128)(2,1)S(1)}, u32[]{:S(2)}) copy-start(bf16[4,128,256]{2,1,0:T(8,128)(2,1)S(1)} %collective-permute-done.2) | copy-start | bytes 786436
  94.9 9.1 %collective-permute-start.3 = (bf16[4,128,256]{2,1,0:T(8,128)(2,1)S(1)}, bf16[4,128,256]{2,1,0:T(8,128)(2,1)S(1)}, u32[]{:S(2)}, u32[]{:S(2)}) collective-permute-start(bf16[4,128,256]{2,1,0:T(8,128)(2,1)S(1)} %collective-permute-done.2), channel_id=1, source_target_pairs={{0,4},{4,8},{8,12},{12,16},{16,20},{20,24},{24,28},{28,0},{1,5},{5... | collective-permute-start | bytes 786440 | tf_op jit(solution)/shard_map/ppermute | solution.py:17
  94.9 229.5 %reduce-scatter.17.cloned.1.call-start = ((), (), s32[]{:S(2)}) async-start(), calls=%async_computation.18 | async-start | bytes 1638400 | tf_op jit(solution)/shard_map/reduce_scatter | solution.py:300
  104.0 19.6 %copy-start.37 = (bf16[4,128,256]{2,1,0:T(8,128)(2,1)}, bf16[4,128,256]{2,1,0:T(8,128)(2,1)S(1)}, u32[]{:S(2)}) copy-start(bf16[4,128,256]{2,1,0:T(8,128)(2,1)S(1)} %collective-permute-done.3) | copy-start | bytes 786436
  104.0 9.1 %collective-permute-start.4 = (bf16[4,128,256]{2,1,0:T(8,128)(2,1)S(1)}, bf16[4,128,256]{2,1,0:T(8,128)(2,1)S(1)}, u32[]{:S(2)}, u32[]{:S(2)}) collective-permute-start(bf16[4,128,256]{2,1,0:T(8,128)(2,1)S(1)} %collective-permute-done.3), channel_id=1, source_target_pairs={{0,4},{4,8},{8,12},{12,16},{16,20},{20,24},{24,28},{28,0},{1,5},{5... | collective-permute-start | bytes 786440 | tf_op jit(solution)/shard_map/ppermute | solution.py:17
  113.0 10.5 %copy-start.39 = (bf16[4,128,256]{2,1,0:T(8,128)(2,1)}, bf16[4,128,256]{2,1,0:T(8,128)(2,1)S(1)}, u32[]{:S(2)}) copy-start(bf16[4,128,256]{2,1,0:T(8,128)(2,1)S(1)} %collective-permute-done.4) | copy-start | bytes 786436
  113.0 9.9 %collective-permute-start.5 = (bf16[4,128,256]{2,1,0:T(8,128)(2,1)S(1)}, bf16[4,128,256]{2,1,0:T(8,128)(2,1)}, u32[]{:S(2)}, u32[]{:S(2)}) collective-permute-start(bf16[4,128,256]{2,1,0:T(8,128)(2,1)S(1)} %collective-permute-done.4), channel_id=1, source_target_pairs={{0,4},{4,8},{8,12},{12,16},{16,20},{20,24},{24,28},{28,0},{1,5},{5... | collective-permute-start | bytes 786440 | tf_op jit(solution)/shard_map/ppermute | solution.py:17
  123.0 9.4 %collective-permute-start.6 = (bf16[4,128,256]{2,1,0:T(8,128)(2,1)}, bf16[4,128,256]{2,1,0:T(8,128)(2,1)}, u32[]{:S(2)}, u32[]{:S(2)}) collective-permute-start(bf16[4,128,256]{2,1,0:T(8,128)(2,1)} %collective-permute-done.5), channel_id=1, source_target_pairs={{0,4},{4,8},{8,12},{12,16},{16,20},{20,24},{24,28},{28,0},{1,5},{5... | collective-permute-start | bytes 786440 | tf_op jit(solution)/shard_map/ppermute | solution.py:17
  123.6 13.9 %copy-start.38 = (bf16[4,128,256]{2,1,0:T(8,128)(2,1)S(1)}, bf16[4,128,256]{2,1,0:T(8,128)(2,1)}, u32[]{:S(2)}) copy-start(bf16[4,128,256]{2,1,0:T(8,128)(2,1)} %copy-done.37) | copy-start | bytes 786436
  123.6 14.6 %copy-start.36 = (bf16[4,128,256]{2,1,0:T(8,128)(2,1)S(1)}, bf16[4,128,256]{2,1,0:T(8,128)(2,1)}, u32[]{:S(2)}) copy-start(bf16[4,128,256]{2,1,0:T(8,128)(2,1)} %copy-done.35) | copy-start | bytes 786436
  123.6 15.3 %copy-start.34 = (bf16[4,128,256]{2,1,0:T(8,128)(2,1)S(1)}, bf16[4,128,256]{2,1,0:T(8,128)(2,1)}, u32[]{:S(2)}) copy-start(bf16[4,128,256]{2,1,0:T(8,128)(2,1)} %copy-done.33) | copy-start | bytes 786436
  135.7 8.8 %copy-start.40 = (bf16[4,128,256]{2,1,0:T(8,128)(2,1)S(1)}, bf16[4,128,256]{2,1,0:T(8,128)(2,1)}, u32[]{:S(2)}) copy-start(bf16[4,128,256]{2,1,0:T(8,128)(2,1)} %copy-done.39) | copy-start | bytes 786436
  197.3 7.1 copy-start.72
  197.3 7.1 copy-start.75
  204.4 5.4 copy-start.41
  231.6 96.9 %reduce-scatter.11.cloned.1.call-start = ((), (), s32[]{:S(2)}) async-start(), calls=%async_computation.15 | async-start | bytes 1638400 | tf_op jit(solution)/shard_map/reduce_scatter | solution.py:291
  303.2 62.4 %reduce-scatter.19.cloned.1.call-start = ((), (), s32[]{:S(2)}) async-start(), calls=%async_computation.19 | async-start | bytes 3276800 | tf_op jit(solution)/shard_map/reduce_scatter | solution.py:303
  307.9 95.1 %reduce-scatter.21.cloned.1.call-start = ((), (), s32[]{:S(2)}) async-start(), calls=%async_computation.20 | async-start | bytes 3276800 | tf_op jit(solution)/shard_map/reduce_scatter | solution.py:306
  313.1 127.1 %reduce-scatter.23.cloned.1.call-start = ((), (), s32[]{:S(2)}) async-start(), calls=%async_computation.21 | async-start | bytes 3276800 | tf_op jit(solution)/shard_map/reduce_scatter | solution.py:309
  319.1 274.6 %reduce-scatter.9.cloned.1.call-start = ((), (), s32[]{:S(2)}) async-start(), calls=%async_computation.14 | async-start | bytes 9437184 | tf_op jit(solution)/shard_map/reduce_scatter | solution.py:268
  319.8 296.2 %reduce-scatter.15.cloned.1.call-start = ((), (), s32[]{:S(2)}) async-start(), calls=%async_computation.17 | async-start | bytes 409600 | tf_op jit(solution)/shard_map/reduce_scatter | solution.py:297
  324.5 271.8 %copy-start.9 = (f32[512,256]{1,0:T(8,128)S(1)}, f32[512,256]{1,0:T(8,128)}, u32[]{:S(2)}) copy-start(f32[512,256]{1,0:T(8,128)} %copy-done.8) | copy-start | bytes 1572868
  324.5 271.8 %copy-start.57 = (f32[4,128]{1,0:T(4,128)S(1)}, f32[4,128]{1,0:T(4,128)}, u32[]{:S(2)}) copy-start(f32[4,128]{1,0:T(4,128)} %copy-done.56) | copy-start | bytes 6148
  324.5 271.8 %copy-start.64 = (f32[256]{0:T(256)S(1)}, f32[256]{0:T(256)}, u32[]{:S(2)}) copy-start(f32[256]{0:T(256)} %copy-done.63) | copy-start | bytes 3076
  596.2 43.4 %reduce-scatter.13.cloned.1.call-start = ((), (), s32[]{:S(2)}) async-start(), calls=%async_computation.16 | async-start | bytes 409600 | tf_op jit(solution)/shard_map/reduce_scatter | solution.py:294
  599.7 10.3 %copy-start.59 = (f32[4,128]{1,0:T(4,128)S(1)}, f32[4,128]{1,0:T(4,128)}, u32[]{:S(2)}) copy-start(f32[4,128]{1,0:T(4,128)} %copy-done.58) | copy-start | bytes 6148
  599.7 10.3 %copy-start.13 = (f32[512,640]{1,0:T(8,128)S(1)}, f32[512,640]{1,0:T(8,128)}, u32[]{:S(2)}) copy-start(f32[512,640]{1,0:T(8,128)} %copy-done.12) | copy-start | bytes 3932164
  609.9 29.7 %copy-start.43 = (bf16[160,2048]{1,0:T(8,128)(2,1)S(1)}, bf16[160,2048]{1,0:T(8,128)(2,1)}, u32[]{:S(2)}) copy-start(bf16[160,2048]{1,0:T(8,128)(2,1)} %reduce-scatter.19.cloned.1.call-done) | copy-start | bytes 1966084
  609.9 29.7 %copy-start.44 = (bf16[160,2048]{1,0:T(8,128)(2,1)S(1)}, bf16[160,2048]{1,0:T(8,128)(2,1)}, u32[]{:S(2)}) copy-start(bf16[160,2048]{1,0:T(8,128)(2,1)} %reduce-scatter.21.cloned.1.call-done) | copy-start | bytes 1966084
  (53 other events, 109.7 us)
Sparse Core Ops, SparseCore 0:
  9.6 22.3 all-gather.8
  35.8 59.6 all-gather.10
  97.1 19.1 all-gather.12
  117.7 25.5 all-gather.14
  144.7 25.5 all-gather.16
  171.7 25.5 all-gather.18
  199.5 49.2 all-gather.20
  251.3 25.0 reduce-scatter.16
  303.4 25.1 reduce-scatter.10
  330.9 34.6 reduce-scatter.18
  368.3 34.6 reduce-scatter.20
  405.4 34.6 reduce-scatter.22
  444.2 149.3 reduce-scatter.8
  596.6 19.4 reduce-scatter.14
  619.1 20.4 reduce-scatter.12
